TPU v7x, 32 devices: a whole 2x2x4 slice. The times are simulated.
32 devices in a mesh: groups: 2 (over y), inst: 4 (over z), tp: 2 (over x), rep: 2 (over core).
Axes of the slice: x: 2, y: 2, z: 4, core: 2. Of those that a mesh axis runs over, the one named last changes fastest.
Arguments:
- queries: bfloat16 [8, 32, 8192], P(('groups', 'rep'), 'inst', 'tp'), parts along dimension 0, may hold values from -8 to 8, as said below
- tool_key_value: bfloat16 [8, 32, 2048], P(('groups', 'rep'), 'inst', 'tp'), parts along dimension 0, may hold values from -8 to 8, as said below
- cache: bfloat16 [8, 3072, 2048], P(('groups', 'rep'), 'inst', 'tp'), parts along dimension 0, may hold values from -6 to 6
- placed: int32 [8, 4], P(('groups', 'rep'), 'inst'), parts along dimension 0, may hold values 0 or 1
- blocks: int32 [8, 4], P(('groups', 'rep'), 'inst'), parts along dimension 0, may hold values from 1 to 6
- span_len: int32 [8], P(('groups', 'rep')), parts along dimension 0, may hold values from 8 to 32
- owner: int32 [8], P(('groups', 'rep')), parts along dimension 0, may hold values from 0 to 3, as said below
Outputs:
- attended: bfloat16 [8, 32, 8192], P(('groups', 'rep'), 'inst', 'tp'), parts along dimension 0
- owned: bfloat16 [8, 2, 32, 2048], P(('groups', 'inst'), 'rep', None, 'tp'), parts along dimension 0
There are 2 independent parts, one for each index of `groups`. A program takes and returns all parts, laid end to end along the dimension named above; each array names one. Nothing has to cross between parts.
Inputs may be any that keep to these rules, and one draw needn't show every extreme that they name: real-valued rotated queries. `tool_key_value`: real-valued rotated keys and values. `owner`: the 2 forks of one index of rep have different owners.
All inputs are finite; a program needn't handle non-finite values. No bound on the sum of `placed` on one device may be relied on, other than what follows from the above.
Results may differ from a plain program's by a relative error of at most 0.0022.
Values may be sent and summed in bfloat16 or wider, within the bound.
A program may use at most 128 MiB of HBM per device.

v0:
```python
import math

import jax
import jax.numpy as jnp
from jax import lax
from jax.sharding import PartitionSpec as P

HEAD_DIM = 128
BLOCK = 128


def passed_along(shard, axis, by):
    size = lax.axis_size(axis)
    return lax.ppermute(shard, axis, [(i, (i + by) % size) for i in range(size)])


def block_partial(query_block, first_token, myself, stores):
    key_cache, value_cache, live_len, key_fresh, value_fresh = stores
    rows_here = query_block.shape[1]
    scaling = 1.0 / math.sqrt(HEAD_DIM)
    score_old = (
        jnp.einsum("fcjgd,fpjd->fcjgp", query_block, key_cache, preferred_element_type=jnp.float32)
        * scaling
    )
    score_new = (
        jnp.einsum("fcjgd,fujd->fcjgu", query_block, key_fresh, preferred_element_type=jnp.float32)
        * scaling
    )
    slots = jnp.arange(key_cache.shape[1], dtype=jnp.int32)
    mask_old = (slots[None, :] < live_len[:, None])[:, None, None, None, :]
    query_token = first_token + jnp.arange(rows_here, dtype=jnp.int32)
    key_token = myself * key_fresh.shape[1] + jnp.arange(key_fresh.shape[1], dtype=jnp.int32)
    mask_new = (key_token[None, :] <= query_token[:, None])[None, :, None, None, :]
    highest = jnp.maximum(
        jnp.max(jnp.where(mask_old, score_old, -jnp.inf), axis=-1),
        jnp.max(jnp.where(mask_new, score_new, -jnp.inf), axis=-1),
    )
    safe_max = jnp.where(highest > -jnp.inf, highest, 0.0)
    weight_old = jnp.where(mask_old, jnp.exp(score_old - safe_max[..., None]), 0.0)
    weight_new = jnp.where(mask_new, jnp.exp(score_new - safe_max[..., None]), 0.0)
    total = jnp.sum(weight_old, axis=-1) + jnp.sum(weight_new, axis=-1)
    numer = jnp.einsum(
        "fcjgp,fpjd->fcjgd",
        weight_old.astype(jnp.bfloat16),
        value_cache,
        preferred_element_type=jnp.float32,
    )
    numer = numer + jnp.einsum(
        "fcjgu,fujd->fcjgd",
        weight_new.astype(jnp.bfloat16),
        value_fresh,
        preferred_element_type=jnp.float32,
    )
    return (highest, total, numer)


def merge_parts(first, second):
    max_one, sum_one, acc_one = first
    max_two, sum_two, acc_two = second
    highest = jnp.maximum(max_one, max_two)
    safe_max = jnp.where(highest > -jnp.inf, highest, 0.0)
    scale_one = jnp.exp(max_one - safe_max)
    scale_two = jnp.exp(max_two - safe_max)
    return (
        highest,
        scale_one * sum_one + scale_two * sum_two,
        scale_one[..., None] * acc_one + scale_two[..., None] * acc_two,
    )


def body(queries, tool_key_value, cache, placed, blocks, span_len, owner):
    forks_here, tokens_here, width_kv = tool_key_value.shape
    kv_heads = width_kv // (2 * HEAD_DIM)
    query_group_size = queries.shape[2] // (kv_heads * HEAD_DIM)
    myself = lax.axis_index("inst")
    members = lax.axis_size("inst")
    query_block = queries.reshape(forks_here, tokens_here, kv_heads, query_group_size, HEAD_DIM)
    stored = cache.reshape(forks_here, cache.shape[1], kv_heads, 2, HEAD_DIM)
    fresh = tool_key_value.reshape(forks_here, tokens_here, kv_heads, 2, HEAD_DIM)
    live_len = placed[:, 0] * blocks[:, 0] * BLOCK
    stores = (
        stored[:, :, :, 0, :],
        stored[:, :, :, 1, :],
        live_len,
        fresh[:, :, :, 0, :],
        fresh[:, :, :, 1, :],
    )
    initial = block_partial(query_block, myself * tokens_here, myself, stores)

    def advance(turn_no, carry):
        moving, running = carry
        moving = passed_along(moving, "inst", 1)
        running = passed_along((running[0], running[1], running[2]), "inst", 1)
        anchor = (myself - turn_no) % members
        return (
            moving,
            merge_parts(running, block_partial(moving, anchor * tokens_here, myself, stores)),
        )

    _, running = lax.fori_loop(1, members, advance, (query_block, initial))
    running = passed_along((running[0], running[1], running[2]), "inst", 1)
    total = running[1]
    numer = running[2]
    token_ids = myself * tokens_here + jnp.arange(tokens_here, dtype=jnp.int32)
    valid = token_ids[None, :] < span_len[:, None]
    result = numer / total[..., None]
    result = jnp.where(valid[:, :, None, None, None], result, 0.0)
    attended = result.reshape(forks_here, tokens_here, queries.shape[2]).astype(jnp.bfloat16)
    kept = jnp.where(valid[:, :, None], tool_key_value, jnp.zeros((), jnp.bfloat16))
    chosen = (owner[None, :] == jnp.arange(members, dtype=jnp.int32)[:, None]).astype(jnp.bfloat16)
    parcels = jnp.einsum("nf,fck->nck", chosen, kept, preferred_element_type=jnp.float32).astype(
        jnp.bfloat16
    )
    arrived = lax.all_to_all(parcels, "inst", split_axis=0, concat_axis=0, tiled=True)
    owned = arrived.reshape(1, 1, members * tokens_here, width_kv)
    return (attended, owned)


def solution(mesh):
    return jax.shard_map(
        body,
        mesh=mesh,
        in_specs=(
            P(("groups", "rep"), "inst", "tp"),
            P(("groups", "rep"), "inst", "tp"),
            P(("groups", "rep"), "inst", "tp"),
            P(("groups", "rep"), "inst"),
            P(("groups", "rep"), "inst"),
            P(("groups", "rep")),
            P(("groups", "rep")),
        ),
        out_specs=(P(("groups", "rep"), "inst", "tp"), P(("groups", "inst"), "rep", None, "tp")),
        check_vma=False,
    )
```

profile of v0, /device:TPU:0, one launch (start us, length us, event | category | flops | bytes accessed | tf_op | source)
XLA Modules:
  0.0 79.1 jit_solution(2424565837753614665)
XLA Ops:
  0.7 0.6 copy-done.4
  1.3 0.7 multiply_bitcast_fusion
  2.1 3.3 %copy.27 = bf16[2,768,1024]{1,2,0:T(8,128)(2,1)S(1)} copy(bf16[2,768,1024]{2,1,0:T(8,128)(2,1)} %param.11) | data formatting | bytes 6291456 | tf_op args[2]
  5.4 0.7 select_reduce_fusion.1
  6.1 0.5 fusion.42
  6.5 0.6 compare_select_fusion.2
  7.2 0.3 fusion.63
  7.6 1.9 %fusion.83 = (bf16[2,768,4,1,128]{1,4,3,2,0:T(8,128)(2,1)}, bf16[2,768,4,1,128]{1,4,3,2,0:T(8,128)(2,1)}) fusion(bf16[2,768,4,2,128]{1,4,3,2,0:T(8,128)(2,1)S(1)} %bitcast.160), kind=kLoop, calls=%fused_computation.95 | loop fusion | bytes 6291456 | tf_op jit(solution)/shard_map/slice | solution.py:83
  9.6 0.6 slice_bitcast_fusion
  10.2 0.4 fusion.49
  10.6 1.5 %fusion.53 = f32[2,8,4,8,128]{4,3,1,2,0:T(8,128)} fusion(f32[2,4,8,8,128]{4,3,2,1,0:T(8,128)S(1)} %fusion.63, f32[2,4,768,8,8]{2,4,3,1,0:T(8,128)S(1)} %get-tuple-element.341, f32[2,8,4,8]{3,1,2,0:T(8,128)S(1)} %get-tuple-element.330, pred[2,768]{1,0:T(4,128)(4,1)S(1)} %iota_compare_fusion.1, bf16[2,768,4,2,128]{1,4,3,2,0:T(8,128)(2,1)S(1)} %bitcast.161), kind=kOutput, calls=%fused_computation.54 | convolution fusion | flops 101908480 | bytes 3705856 | tf_op jit(solution)/shard_map/fcjgp,fpjd->fcjgd/dot_general | solution.py:42
  12.1 1.9 %copy.49 = bf16[2,768,4,1,128]{4,1,2,0,3:T(8,128)(2,1)S(1)} copy(bf16[2,768,4,1,128]{1,4,3,2,0:T(8,128)(2,1)} %get-tuple-element.337) | data formatting | bytes 3145728
  14.0 1.9 %copy.51 = bf16[2,768,4,1,128]{4,1,2,0,3:T(8,128)(2,1)S(1)} copy(bf16[2,768,4,1,128]{1,4,3,2,0:T(8,128)(2,1)} %get-tuple-element.336) | data formatting | bytes 3145728
  15.9 0.7 copy.35
  16.6 0.6 add.141
  17.2 45.7 %while.21 = (s32[]{:T(128)}, bf16[2,8,4,8,128]{4,3,1,2,0:T(8,128)(2,1)}, f32[2,8,4,8]{3,1,2,0:T(8,128)}, f32[2,8,4,8]{3,1,2,0:T(8,128)}, f32[2,8,4,8,128]{4,3,1,...) while((s32[]{:T(128)}, ...), condition=%wide.region_9.10_spmd, body=%wide.region_4.9_spmd.sunk | while | flops 207267408 | bytes 11228014 | solution.py:100
  17.2 3.0 %collective-permute-start = (bf16[2,8,4,8,128]{4,3,1,2,0:T(8,128)(2,1)}, bf16[2,8,4,8,128]{4,3,1,2,0:T(8,128)(2,1)S(1)}, u32[]{:S(2)}, u32[]{:S(2)}) collective-permute-start(bf16[2,8,4,8,128]{4,3,1,2,0:T(8,128)(2,1)} %get-tuple-element.455), channel_id=1, source_target_pairs={{0,4},{4,8},{8,12},{12,0},{1,5},{5,9},{9,13},{13,1},{2,6},{6,10},{... | collective-permute-start | bytes 393224 | tf_op jit(solution)/shard_map/while/body/eval_jaxpr/ppermute | solution.py:14
  20.2 1.6 %collective-permute-start.1 = (f32[2,8,4,8]{3,1,2,0:T(8,128)}, f32[2,8,4,8]{3,1,2,0:T(8,128)}, u32[]{:S(2)}, u32[]{:S(2)}) collective-permute-start(f32[2,8,4,8]{3,1,2,0:T(8,128)} %get-tuple-element.457), channel_id=1, source_target_pairs={{0,4},{4,8},{8,12},{12,0},{1,5},{5,9},{9,13},{13,1},{2,6},{6,10},{... | collective-permute-start | bytes 6152 | tf_op jit(solution)/shard_map/while/body/eval_jaxpr/ppermute | solution.py:14
  21.8 1.6 %collective-permute-start.2 = (f32[2,8,4,8]{3,1,2,0:T(8,128)}, f32[2,8,4,8]{3,1,2,0:T(8,128)}, u32[]{:S(2)}, u32[]{:S(2)}) collective-permute-start(f32[2,8,4,8]{3,1,2,0:T(8,128)} %get-tuple-element.456), channel_id=1, source_target_pairs={{0,4},{4,8},{8,12},{12,0},{1,5},{5,9},{9,13},{13,1},{2,6},{6,10},{... | collective-permute-start | bytes 6152 | tf_op jit(solution)/shard_map/while/body/eval_jaxpr/ppermute | solution.py:14
  23.4 0.7 iota_compare_fusion.3
  24.2 2.5 %collective-permute-done = bf16[2,8,4,8,128]{4,3,1,2,0:T(8,128)(2,1)S(1)} collective-permute-done((bf16[2,8,4,8,128]{4,3,1,2,0:T(8,128)(2,1)}, bf16[2,8,4,8,128]{4,3,1,2,0:T(8,128)(2,1)S(1)}, u32[]{:S(2)}, u32[]{:S(2)}) %collective-permute-start) | collective-permute-done | bytes 131104 | tf_op jit(solution)/shard_map/while/body/eval_jaxpr/ppermute | solution.py:14
  26.6 0.7 select_reduce_fusion.3
  27.4 0.7 fusion.102
  28.1 0.4 fusion.103
  28.7 1.4 %multiply_add_fusion.4 = (f32[2,8,4,8]{3,1,2,0:T(8,128)}, f32[2,8,4,8]{3,1,2,0:T(8,128)S(1)}, f32[2,8,4,8]{3,1,2,0:T(8,128)S(1)}, f32[2,8,4,8]{3,1,2,0:T(8,128)}) fusion(f32[2,8,4,8]{3,1,2,0:T(8,128)S(1)} %fusion.103, f32[2,8,4,8]{3,1,2,0:T(8,128)S(1)} %fusion.104, f32[2,8,4,8]{3,1,2,0:T(8,128)} %collective-permute-done.1, ...), kind=kLoop, calls=%fused_computation.30.clone.1 | loop fusion | flops 4608 | bytes 18432 | tf_op jit(solution)/shard_map/while/body/eval_jaxpr/add | solution.py:66
  30.1 0.7 copy.81
  30.8 0.3 fusion.105
  31.1 1.9 %collective-permute-done.3 = f32[2,8,4,8,128]{4,3,1,2,0:T(8,128)S(1)} collective-permute-done((f32[2,8,4,8,128]{4,3,1,2,0:T(8,128)}, f32[2,8,4,8,128]{4,3,1,2,0:T(8,128)S(1)}, u32[]{:S(2)}, u32[]{:S(2)}) %collective-permute-start.3) | collective-permute-done | bytes 262176 | tf_op jit(solution)/shard_map/while/body/eval_jaxpr/ppermute | solution.py:14
  33.0 1.2 %multiply_add_fusion.5 = f32[2,8,4,8,128]{4,3,1,2,0:T(8,128)} fusion(f32[2,8,4,8,128]{4,3,1,2,0:T(8,128)S(1)} %collective-permute-done.3, f32[2,8,4,8]{3,1,2,0:T(8,128)S(1)} %get-tuple-element.435, f32[2,8,4,8]{3,1,2,0:T(8,128)S(1)} %get-tuple-element.436, f32[2,4,8,8,128]{4,3,2,1,0:T(8,128)S(1)} %fusion.105, ...), kind=kOutput, calls=%fused_computation.19.clone.1 | convolution fusion | flops 102105088 | bytes 3939840 | tf_op jit(solution)/shard_map/while/body/eval_jaxpr/fcjgp,fpjd->fcjgd/dot_general | solution.py:42
  34.2 1.3 %collective-permute-start.1 = (f32[2,8,4,8]{3,1,2,0:T(8,128)}, f32[2,8,4,8]{3,1,2,0:T(8,128)}, u32[]{:S(2)}, u32[]{:S(2)}) collective-permute-start(f32[2,8,4,8]{3,1,2,0:T(8,128)} %get-tuple-element.457), channel_id=1, source_target_pairs={{0,4},{4,8},{8,12},{12,0},{1,5},{5,9},{9,13},{13,1},{2,6},{6,10},{... | collective-permute-start | bytes 6152 | tf_op jit(solution)/shard_map/while/body/eval_jaxpr/ppermute | solution.py:14
  35.5 1.6 %collective-permute-start.2 = (f32[2,8,4,8]{3,1,2,0:T(8,128)}, f32[2,8,4,8]{3,1,2,0:T(8,128)}, u32[]{:S(2)}, u32[]{:S(2)}) collective-permute-start(f32[2,8,4,8]{3,1,2,0:T(8,128)} %get-tuple-element.456), channel_id=1, source_target_pairs={{0,4},{4,8},{8,12},{12,0},{1,5},{5,9},{9,13},{13,1},{2,6},{6,10},{... | collective-permute-start | bytes 6152 | tf_op jit(solution)/shard_map/while/body/eval_jaxpr/ppermute | solution.py:14
  37.1 2.1 %collective-permute-start.3 = (f32[2,8,4,8,128]{4,3,1,2,0:T(8,128)}, f32[2,8,4,8,128]{4,3,1,2,0:T(8,128)S(1)}, u32[]{:S(2)}, u32[]{:S(2)}) collective-permute-start(f32[2,8,4,8,128]{4,3,1,2,0:T(8,128)} %get-tuple-element.458), channel_id=1, source_target_pairs={{0,4},{4,8},{8,12},{12,0},{1,5},{5,9},{9,13},{13,1},{2,6},{6,10},{... | collective-permute-start | bytes 786440 | tf_op jit(solution)/shard_map/while/body/eval_jaxpr/ppermute | solution.py:14
  39.2 0.7 iota_compare_fusion.3
  39.9 2.6 %collective-permute-done = bf16[2,8,4,8,128]{4,3,1,2,0:T(8,128)(2,1)S(1)} collective-permute-done((bf16[2,8,4,8,128]{4,3,1,2,0:T(8,128)(2,1)}, bf16[2,8,4,8,128]{4,3,1,2,0:T(8,128)(2,1)S(1)}, u32[]{:S(2)}, u32[]{:S(2)}) %collective-permute-start) | collective-permute-done | bytes 131104 | tf_op jit(solution)/shard_map/while/body/eval_jaxpr/ppermute | solution.py:14
  42.6 0.7 select_reduce_fusion.3
  43.3 0.7 fusion.102
  44.0 0.4 fusion.103
  44.6 1.4 %multiply_add_fusion.4 = (f32[2,8,4,8]{3,1,2,0:T(8,128)}, f32[2,8,4,8]{3,1,2,0:T(8,128)S(1)}, f32[2,8,4,8]{3,1,2,0:T(8,128)S(1)}, f32[2,8,4,8]{3,1,2,0:T(8,128)}) fusion(f32[2,8,4,8]{3,1,2,0:T(8,128)S(1)} %fusion.103, f32[2,8,4,8]{3,1,2,0:T(8,128)S(1)} %fusion.104, f32[2,8,4,8]{3,1,2,0:T(8,128)} %collective-permute-done.1, ...), kind=kLoop, calls=%fused_computation.30.clone.1 | loop fusion | flops 4608 | bytes 18432 | tf_op jit(solution)/shard_map/while/body/eval_jaxpr/add | solution.py:66
  46.0 0.7 copy.81
  46.7 0.3 fusion.105
  47.0 0.5 collective-permute-done.3
  47.5 1.2 %multiply_add_fusion.5 = f32[2,8,4,8,128]{4,3,1,2,0:T(8,128)} fusion(f32[2,8,4,8,128]{4,3,1,2,0:T(8,128)S(1)} %collective-permute-done.3, f32[2,8,4,8]{3,1,2,0:T(8,128)S(1)} %get-tuple-element.435, f32[2,8,4,8]{3,1,2,0:T(8,128)S(1)} %get-tuple-element.436, f32[2,4,8,8,128]{4,3,2,1,0:T(8,128)S(1)} %fusion.105, ...), kind=kOutput, calls=%fused_computation.19.clone.1 | convolution fusion | flops 102105088 | bytes 3939840 | tf_op jit(solution)/shard_map/while/body/eval_jaxpr/fcjgp,fpjd->fcjgd/dot_general | solution.py:42
  48.8 1.2 %collective-permute-start.2 = (f32[2,8,4,8]{3,1,2,0:T(8,128)}, f32[2,8,4,8]{3,1,2,0:T(8,128)}, u32[]{:S(2)}, u32[]{:S(2)}) collective-permute-start(f32[2,8,4,8]{3,1,2,0:T(8,128)} %get-tuple-element.456), channel_id=1, source_target_pairs={{0,4},{4,8},{8,12},{12,0},{1,5},{5,9},{9,13},{13,1},{2,6},{6,10},{... | collective-permute-start | bytes 6152 | tf_op jit(solution)/shard_map/while/body/eval_jaxpr/ppermute | solution.py:14
  49.9 3.8 %collective-permute-start.3 = (f32[2,8,4,8,128]{4,3,1,2,0:T(8,128)}, f32[2,8,4,8,128]{4,3,1,2,0:T(8,128)S(1)}, u32[]{:S(2)}, u32[]{:S(2)}) collective-permute-start(f32[2,8,4,8,128]{4,3,1,2,0:T(8,128)} %get-tuple-element.458), channel_id=1, source_target_pairs={{0,4},{4,8},{8,12},{12,0},{1,5},{5,9},{9,13},{13,1},{2,6},{6,10},{... | collective-permute-start | bytes 786440 | tf_op jit(solution)/shard_map/while/body/eval_jaxpr/ppermute | solution.py:14
  53.7 0.7 iota_compare_fusion.3
  54.5 2.7 %collective-permute-done = bf16[2,8,4,8,128]{4,3,1,2,0:T(8,128)(2,1)S(1)} collective-permute-done((bf16[2,8,4,8,128]{4,3,1,2,0:T(8,128)(2,1)}, bf16[2,8,4,8,128]{4,3,1,2,0:T(8,128)(2,1)S(1)}, u32[]{:S(2)}, u32[]{:S(2)}) %collective-permute-start) | collective-permute-done | bytes 131104 | tf_op jit(solution)/shard_map/while/body/eval_jaxpr/ppermute | solution.py:14
  57.2 0.7 select_reduce_fusion.3
  57.9 0.7 fusion.102
  58.7 0.4 fusion.103
  59.3 1.4 %multiply_add_fusion.4 = (f32[2,8,4,8]{3,1,2,0:T(8,128)}, f32[2,8,4,8]{3,1,2,0:T(8,128)S(1)}, f32[2,8,4,8]{3,1,2,0:T(8,128)S(1)}, f32[2,8,4,8]{3,1,2,0:T(8,128)}) fusion(f32[2,8,4,8]{3,1,2,0:T(8,128)S(1)} %fusion.103, f32[2,8,4,8]{3,1,2,0:T(8,128)S(1)} %fusion.104, f32[2,8,4,8]{3,1,2,0:T(8,128)} %collective-permute-done.1, ...), kind=kLoop, calls=%fused_computation.30.clone.1 | loop fusion | flops 4608 | bytes 18432 | tf_op jit(solution)/shard_map/while/body/eval_jaxpr/add | solution.py:66
  60.7 0.7 copy.81
  61.3 0.3 fusion.105
  61.6 1.2 %multiply_add_fusion.5 = f32[2,8,4,8,128]{4,3,1,2,0:T(8,128)} fusion(f32[2,8,4,8,128]{4,3,1,2,0:T(8,128)S(1)} %collective-permute-done.3, f32[2,8,4,8]{3,1,2,0:T(8,128)S(1)} %get-tuple-element.435, f32[2,8,4,8]{3,1,2,0:T(8,128)S(1)} %get-tuple-element.436, f32[2,4,8,8,128]{4,3,2,1,0:T(8,128)S(1)} %fusion.105, ...), kind=kOutput, calls=%fused_computation.19.clone.1 | convolution fusion | flops 102105088 | bytes 3939840 | tf_op jit(solution)/shard_map/while/body/eval_jaxpr/fcjgp,fpjd->fcjgd/dot_general | solution.py:42
  62.9 0.7 broadcast_compare_fusion.2
  63.6 0.8 %broadcast_select_fusion = bf16[2,8,1024]{2,1,0:T(8,128)(2,1)S(1)} fusion(bf16[2,8,1024]{2,1,0:T(8,128)(2,1)} %param.10, pred[2,8]{1,0:T(4,128)(4,1)S(1)} %broadcast_compare_fusion.2), kind=kLoop, calls=%fused_computation.73 | loop fusion | flops 16384 | bytes 65552 | tf_op jit(solution)/shard_map/jit(_where)/select_n | solution.py:109
  64.5 0.9 %convolution_convert_fusion = bf16[4,8,1024]{2,0,1:T(4,128)(2,1)S(1)} fusion(bf16[2,8,1024]{2,1,0:T(8,128)(2,1)S(1)} %broadcast_select_fusion, s32[2]{0:T(128)} %param.15), kind=kOutput, calls=%fused_computation.57 | convolution fusion | flops 163848 | bytes 98312 | tf_op jit(solution)/shard_map/nf,fck->nck/dot_general | solution.py:111
  65.4 0.7 copy.38
  66.1 5.1 %all-to-all-start = ((bf16[4,8,1024]{2,1,0:T(8,128)(2,1)}), bf16[4,8,1024]{2,1,0:T(8,128)(2,1)S(1)}, u32[]{:S(2)}, u32[]{:S(2)}) async-start(bf16[4,8,1024]{2,1,0:T(8,128)(2,1)} %copy.38), calls=%async_computation | async-start | bytes 131072 | tf_op jit(solution)/shard_map/all_to_all | solution.py:114
  71.2 2.0 %collective-permute-start.5 = (f32[2,8,4,8]{3,1,2,0:T(8,128)}, f32[2,8,4,8]{3,1,2,0:T(8,128)S(1)}, u32[]{:S(2)}, u32[]{:S(2)}) collective-permute-start(f32[2,8,4,8]{3,1,2,0:T(8,128)} %get-tuple-element.275), channel_id=1, source_target_pairs={{0,4},{4,8},{8,12},{12,0},{1,5},{5,9},{9,13},{13,1},{2,6},{6,10},{... | collective-permute-start | bytes 6152 | tf_op jit(solution)/shard_map/ppermute | solution.py:14
  73.2 3.7 %all-to-all-done = bf16[4,8,1024]{2,1,0:T(8,128)(2,1)S(1)} async-done(((bf16[4,8,1024]{2,1,0:T(8,128)(2,1)}), bf16[4,8,1024]{2,1,0:T(8,128)(2,1)S(1)}, u32[]{:S(2)}, u32[]{:S(2)}) %all-to-all-start) | async-done | bytes 65568 | tf_op jit(solution)/shard_map/all_to_all | solution.py:114
  76.9 0.7 collective-permute-done.5
  77.6 0.2 select_convert_fusion
  77.8 0.7 copy.36
  78.5 0.6 copy.86
  (46 shorter events, 1.1 us)
Async XLA Ops:
  0.6 0.6 copy-start.4
  2.0 3.3 %copy-start.3 = (s32[2]{0:T(128)}, s32[2]{0:T(128)S(1)}, u32[]{:S(2)}) copy-start(s32[2]{0:T(128)S(1)} %multiply_bitcast_fusion) | copy-start | bytes 28
  2.1 3.3 %copy-start.1 = (bf16[2,8,1024]{2,1,0:T(8,128)(2,1)S(1)}, bf16[2,8,1024]{2,1,0:T(8,128)(2,1)}, u32[]{:S(2)}) copy-start(bf16[2,8,1024]{2,1,0:T(8,128)(2,1)} %param.10) | copy-start | bytes 98308
  2.1 3.3 %copy-start.2 = (bf16[2,8,4096]{2,1,0:T(8,128)(2,1)S(1)}, bf16[2,8,4096]{2,1,0:T(8,128)(2,1)}, u32[]{:S(2)}) copy-start(bf16[2,8,4096]{2,1,0:T(8,128)(2,1)} %param.9) | copy-start | bytes 393220
  17.2 9.5 %collective-permute-start = (bf16[2,8,4,8,128]{4,3,1,2,0:T(8,128)(2,1)}, bf16[2,8,4,8,128]{4,3,1,2,0:T(8,128)(2,1)S(1)}, u32[]{:S(2)}, u32[]{:S(2)}) collective-permute-start(bf16[2,8,4,8,128]{4,3,1,2,0:T(8,128)(2,1)} %get-tuple-element.455), channel_id=1, source_target_pairs={{0,4},{4,8},{8,12},{12,0},{1,5},{5,9},{9,13},{13,1},{2,6},{6,10},{... | collective-permute-start | bytes 393224 | tf_op jit(solution)/shard_map/while/body/eval_jaxpr/ppermute | solution.py:14
  20.2 8.5 %collective-permute-start.1 = (f32[2,8,4,8]{3,1,2,0:T(8,128)}, f32[2,8,4,8]{3,1,2,0:T(8,128)}, u32[]{:S(2)}, u32[]{:S(2)}) collective-permute-start(f32[2,8,4,8]{3,1,2,0:T(8,128)} %get-tuple-element.457), channel_id=1, source_target_pairs={{0,4},{4,8},{8,12},{12,0},{1,5},{5,9},{9,13},{13,1},{2,6},{6,10},{... | collective-permute-start | bytes 6152 | tf_op jit(solution)/shard_map/while/body/eval_jaxpr/ppermute | solution.py:14
  21.8 6.9 %collective-permute-start.2 = (f32[2,8,4,8]{3,1,2,0:T(8,128)}, f32[2,8,4,8]{3,1,2,0:T(8,128)}, u32[]{:S(2)}, u32[]{:S(2)}) collective-permute-start(f32[2,8,4,8]{3,1,2,0:T(8,128)} %get-tuple-element.456), channel_id=1, source_target_pairs={{0,4},{4,8},{8,12},{12,0},{1,5},{5,9},{9,13},{13,1},{2,6},{6,10},{... | collective-permute-start | bytes 6152 | tf_op jit(solution)/shard_map/while/body/eval_jaxpr/ppermute | solution.py:14
  23.4 9.6 %collective-permute-start.3 = (f32[2,8,4,8,128]{4,3,1,2,0:T(8,128)}, f32[2,8,4,8,128]{4,3,1,2,0:T(8,128)S(1)}, u32[]{:S(2)}, u32[]{:S(2)}) collective-permute-start(f32[2,8,4,8,128]{4,3,1,2,0:T(8,128)} %get-tuple-element.458), channel_id=1, source_target_pairs={{0,4},{4,8},{8,12},{12,0},{1,5},{5,9},{9,13},{13,1},{2,6},{6,10},{... | collective-permute-start | bytes 786440 | tf_op jit(solution)/shard_map/while/body/eval_jaxpr/ppermute | solution.py:14
  28.1 2.7 %copy-start = (bf16[2,8,4,128]{3,1,2,0:T(8,128)(2,1)S(1)}, bf16[2,8,4,128]{3,1,2,0:T(8,128)(2,1)}, u32[]{:S(2)}) copy-start(bf16[2,8,4,128]{3,1,2,0:T(8,128)(2,1)} %get-tuple-element.482) | copy-start | bytes 49156 | tf_op jit(solution)/shard_map/while
  34.2 8.4 %collective-permute-start = (bf16[2,8,4,8,128]{4,3,1,2,0:T(8,128)(2,1)}, bf16[2,8,4,8,128]{4,3,1,2,0:T(8,128)(2,1)S(1)}, u32[]{:S(2)}, u32[]{:S(2)}) collective-permute-start(bf16[2,8,4,8,128]{4,3,1,2,0:T(8,128)(2,1)} %get-tuple-element.455), channel_id=1, source_target_pairs={{0,4},{4,8},{8,12},{12,0},{1,5},{5,9},{9,13},{13,1},{2,6},{6,10},{... | collective-permute-start | bytes 393224 | tf_op jit(solution)/shard_map/while/body/eval_jaxpr/ppermute | solution.py:14
  34.2 10.4 %collective-permute-start.1 = (f32[2,8,4,8]{3,1,2,0:T(8,128)}, f32[2,8,4,8]{3,1,2,0:T(8,128)}, u32[]{:S(2)}, u32[]{:S(2)}) collective-permute-start(f32[2,8,4,8]{3,1,2,0:T(8,128)} %get-tuple-element.457), channel_id=1, source_target_pairs={{0,4},{4,8},{8,12},{12,0},{1,5},{5,9},{9,13},{13,1},{2,6},{6,10},{... | collective-permute-start | bytes 6152 | tf_op jit(solution)/shard_map/while/body/eval_jaxpr/ppermute | solution.py:14
  35.5 9.1 %collective-permute-start.2 = (f32[2,8,4,8]{3,1,2,0:T(8,128)}, f32[2,8,4,8]{3,1,2,0:T(8,128)}, u32[]{:S(2)}, u32[]{:S(2)}) collective-permute-start(f32[2,8,4,8]{3,1,2,0:T(8,128)} %get-tuple-element.456), channel_id=1, source_target_pairs={{0,4},{4,8},{8,12},{12,0},{1,5},{5,9},{9,13},{13,1},{2,6},{6,10},{... | collective-permute-start | bytes 6152 | tf_op jit(solution)/shard_map/while/body/eval_jaxpr/ppermute | solution.py:14
  37.1 10.4 %collective-permute-start.3 = (f32[2,8,4,8,128]{4,3,1,2,0:T(8,128)}, f32[2,8,4,8,128]{4,3,1,2,0:T(8,128)S(1)}, u32[]{:S(2)}, u32[]{:S(2)}) collective-permute-start(f32[2,8,4,8,128]{4,3,1,2,0:T(8,128)} %get-tuple-element.458), channel_id=1, source_target_pairs={{0,4},{4,8},{8,12},{12,0},{1,5},{5,9},{9,13},{13,1},{2,6},{6,10},{... | collective-permute-start | bytes 786440 | tf_op jit(solution)/shard_map/while/body/eval_jaxpr/ppermute | solution.py:14
  44.0 2.7 %copy-start = (bf16[2,8,4,128]{3,1,2,0:T(8,128)(2,1)S(1)}, bf16[2,8,4,128]{3,1,2,0:T(8,128)(2,1)}, u32[]{:S(2)}) copy-start(bf16[2,8,4,128]{3,1,2,0:T(8,128)(2,1)} %get-tuple-element.482) | copy-start | bytes 49156 | tf_op jit(solution)/shard_map/while
  48.7 8.4 %collective-permute-start = (bf16[2,8,4,8,128]{4,3,1,2,0:T(8,128)(2,1)}, bf16[2,8,4,8,128]{4,3,1,2,0:T(8,128)(2,1)S(1)}, u32[]{:S(2)}, u32[]{:S(2)}) collective-permute-start(bf16[2,8,4,8,128]{4,3,1,2,0:T(8,128)(2,1)} %get-tuple-element.455), channel_id=1, source_target_pairs={{0,4},{4,8},{8,12},{12,0},{1,5},{5,9},{9,13},{13,1},{2,6},{6,10},{... | collective-permute-start | bytes 393224 | tf_op jit(solution)/shard_map/while/body/eval_jaxpr/ppermute | solution.py:14
  48.7 10.5 %collective-permute-start.1 = (f32[2,8,4,8]{3,1,2,0:T(8,128)}, f32[2,8,4,8]{3,1,2,0:T(8,128)}, u32[]{:S(2)}, u32[]{:S(2)}) collective-permute-start(f32[2,8,4,8]{3,1,2,0:T(8,128)} %get-tuple-element.457), channel_id=1, source_target_pairs={{0,4},{4,8},{8,12},{12,0},{1,5},{5,9},{9,13},{13,1},{2,6},{6,10},{... | collective-permute-start | bytes 6152 | tf_op jit(solution)/shard_map/while/body/eval_jaxpr/ppermute | solution.py:14
  48.8 10.5 %collective-permute-start.2 = (f32[2,8,4,8]{3,1,2,0:T(8,128)}, f32[2,8,4,8]{3,1,2,0:T(8,128)}, u32[]{:S(2)}, u32[]{:S(2)}) collective-permute-start(f32[2,8,4,8]{3,1,2,0:T(8,128)} %get-tuple-element.456), channel_id=1, source_target_pairs={{0,4},{4,8},{8,12},{12,0},{1,5},{5,9},{9,13},{13,1},{2,6},{6,10},{... | collective-permute-start | bytes 6152 | tf_op jit(solution)/shard_map/while/body/eval_jaxpr/ppermute | solution.py:14
  49.9 11.7 %collective-permute-start.3 = (f32[2,8,4,8,128]{4,3,1,2,0:T(8,128)}, f32[2,8,4,8,128]{4,3,1,2,0:T(8,128)S(1)}, u32[]{:S(2)}, u32[]{:S(2)}) collective-permute-start(f32[2,8,4,8,128]{4,3,1,2,0:T(8,128)} %get-tuple-element.458), channel_id=1, source_target_pairs={{0,4},{4,8},{8,12},{12,0},{1,5},{5,9},{9,13},{13,1},{2,6},{6,10},{... | collective-permute-start | bytes 786440 | tf_op jit(solution)/shard_map/while/body/eval_jaxpr/ppermute | solution.py:14
  58.6 2.7 %copy-start = (bf16[2,8,4,128]{3,1,2,0:T(8,128)(2,1)S(1)}, bf16[2,8,4,128]{3,1,2,0:T(8,128)(2,1)}, u32[]{:S(2)}) copy-start(bf16[2,8,4,128]{3,1,2,0:T(8,128)(2,1)} %get-tuple-element.482) | copy-start | bytes 49156 | tf_op jit(solution)/shard_map/while
  62.9 14.7 %collective-permute-start.4 = (f32[2,8,4,8,128]{4,3,1,2,0:T(8,128)}, f32[2,8,4,8,128]{4,3,1,2,0:T(8,128)S(1)}, u32[]{:S(2)}, u32[]{:S(2)}) collective-permute-start(f32[2,8,4,8,128]{4,3,1,2,0:T(8,128)} %get-tuple-element.274), channel_id=1, source_target_pairs={{0,4},{4,8},{8,12},{12,0},{1,5},{5,9},{9,13},{13,1},{2,6},{6,10},{... | collective-permute-start | bytes 786440 | tf_op jit(solution)/shard_map/ppermute | solution.py:14
  66.1 10.8 %all-to-all-start = ((bf16[4,8,1024]{2,1,0:T(8,128)(2,1)}), bf16[4,8,1024]{2,1,0:T(8,128)(2,1)S(1)}, u32[]{:S(2)}, u32[]{:S(2)}) async-start(bf16[4,8,1024]{2,1,0:T(8,128)(2,1)} %copy.38), calls=%async_computation | async-start | bytes 131072 | tf_op jit(solution)/shard_map/all_to_all | solution.py:114
  71.2 6.4 %collective-permute-start.5 = (f32[2,8,4,8]{3,1,2,0:T(8,128)}, f32[2,8,4,8]{3,1,2,0:T(8,128)S(1)}, u32[]{:S(2)}, u32[]{:S(2)}) collective-permute-start(f32[2,8,4,8]{3,1,2,0:T(8,128)} %get-tuple-element.275), channel_id=1, source_target_pairs={{0,4},{4,8},{8,12},{12,0},{1,5},{5,9},{9,13},{13,1},{2,6},{6,10},{... | collective-permute-start | bytes 6152 | tf_op jit(solution)/shard_map/ppermute | solution.py:14
where the time goes:
time: 79.7 us; the launch traced here: 79.1 us
  starting transfers between devices  23.2 us (29%)
  local copies, waits for them, and re-layouts  14.8 us (19%)
  waiting for transfers between devices  14.7 us (18%)
  matrix products  12.8 us (16%)
  other arithmetic  12.6 us (16%)
    ppermute x14, starting transfers between devices, passed_along(): lax.ppermute(shard, axis, [(i, (i + by) % size) for i in range(size)])  18.2 us
    ppermute x14, waiting for transfers between devices, passed_along(): lax.ppermute(shard, axis, [(i, (i + by) % size) for i in range(size)])  10.9 us
    unnamed x13, local copies, waits for them, and re-layouts  8.31 us
    dot_general x4, matrix products, block_partial(): jnp.einsum('fcjgp,fpjd->fcjgd', weight_old.astype(jnp.bfloat16), value_ca...  5.18 us
    all_to_all x1, starting transfers between devices, body(): lax.all_to_all(parcels, 'inst', split_axis=0, concat_axis=0, tiled=True)  5.09 us
    add x3, other arithmetic, merge_parts(): scale_one * sum_one + scale_two * sum_two  4.21 us
    all_to_all x1, waiting for transfers between devices, body(): lax.all_to_all(parcels, 'inst', split_axis=0, concat_axis=0, tiled=True)  3.72 us
    dot_general x4, matrix products, block_partial(): jnp.einsum('fcjgd,fujd->fcjgu', query_block, key_fresh, preferred_element...  2.79 us
  transfers between devices with their start and end apart: 15, of which 7 were waited for; matrix products, arithmetic and copies ran while one was open for 23% of the time, Pallas kernels for 0%

commit v1 on v0

v1 whole, which is shorter than its diff:
```python
import functools
import math

import jax
import jax.numpy as jnp
from jax import lax
from jax.experimental import pallas as pl
from jax.experimental.pallas import tpu as pltpu
from jax.sharding import PartitionSpec as P

HEAD_DIM = 128
BLOCK = 128
FRESH_ROWS = 16
CHUNKS = 4
STEPS = 32000.0
LOG2E = 1.4426950408889634
HIDDEN = -1e30
FLOOR = -1e5
MESH = pl.DeviceIdType.MESH
NT = (((1,), (1,)), ((), ()))
TN = (((0,), (0,)), ((), ()))


def kernel(
    n, q_ref, kv_ref, cache_ref, placed_ref, blocks_ref, span_ref, owner_ref,
    att_ref, owned_ref,
    cbuf, vt, kf, vf, qbuf, pn, ps, ci, cis, co, cos, po, pi,
    cache_sem, q_send, q_recv, c_send, s_send, c_recv, s_recv, o_send, o_recv,
):
    forks, tokens, width = q_ref.shape
    width_kv = kv_ref.shape[2]
    kv_heads = width_kv // (2 * HEAD_DIM)
    group = width // (kv_heads * HEAD_DIM)
    rows = group * tokens
    lanes = 2 * rows
    pairs = forks * kv_heads // 2
    slots = cache_ref.shape[1]
    per = pairs // CHUNKS
    factor = LOG2E / math.sqrt(HEAD_DIM)
    me = lax.axis_index("inst")

    fetches = [
        pltpu.make_async_copy(cache_ref.at[f], cbuf.at[f], cache_sem.at[f])
        for f in range(forks)
    ]
    for fetch in fetches:
        fetch.start()

    barrier = pltpu.get_barrier_semaphore()
    for k in range(1, n):
        pl.semaphore_signal(
            barrier, inc=1, device_id={"inst": lax.rem(me + k, n)}, device_id_type=MESH
        )

    def members(p):
        return [(u // kv_heads, u % kv_heads) for u in (2 * p, 2 * p + 1)]

    for p in range(pairs):
        parts = []
        for f, j in members(p):
            for g in range(group):
                at = (j * group + g) * HEAD_DIM
                parts.append(q_ref[f, :, at : at + HEAD_DIM].astype(jnp.float32))
        qbuf[me, p] = jnp.concatenate(parts, axis=0).astype(jnp.bfloat16)

    pl.semaphore_wait(barrier, n - 1)

    def q_copy(origin, c, side):
        part = qbuf.at[origin, pl.ds(c * per, per)]
        return pltpu.make_async_remote_copy(
            src_ref=part, dst_ref=part,
            send_sem=q_send.at[side, origin, c], recv_sem=q_recv.at[origin, c],
            device_id={"inst": me + 1 if side == 0 else me - 1}, device_id_type=MESH,
        )

    for c in range(CHUNKS):
        for side in range(2):
            @pl.when(me + 1 < n if side == 0 else me > 0)
            def _():
                q_copy(me, c, side).start()

    for i in range(n):
        chosen = None
        for f in range(forks):
            tile = kv_ref[f].astype(jnp.float32)
            token = me * tokens + lax.broadcasted_iota(jnp.int32, tile.shape, 0)
            keep = (token < span_ref[f]) & (jnp.broadcast_to(owner_ref[f], tile.shape) == i)
            tile = jnp.where(keep, tile, 0.0)
            chosen = tile if chosen is None else chosen + tile
        po[i] = jnp.concatenate(
            [chosen[:, a : a + HEAD_DIM] for a in range(0, width_kv, HEAD_DIM)], axis=0
        ).astype(jnp.bfloat16)
    pi[me] = po[me]

    def parcel(k):
        target = lax.rem(me + k, n)
        return pltpu.make_async_remote_copy(
            src_ref=po.at[target], dst_ref=pi.at[me],
            send_sem=o_send.at[target], recv_sem=o_recv.at[me],
            device_id={"inst": target}, device_id_type=MESH,
        )

    for k in range(1, n):
        parcel(k).start()

    for p in range(pairs):
        for ref, shift in ((kf, 0), (vf, HEAD_DIM)):
            both = [
                kv_ref[f, :, 2 * j * HEAD_DIM + shift : 2 * j * HEAD_DIM + shift + HEAD_DIM]
                for f, j in members(p)
            ]
            tile = jnp.concatenate(both, axis=1).astype(jnp.float32)
            pad = jnp.zeros((FRESH_ROWS - tokens, 2 * HEAD_DIM), jnp.float32)
            ref[p] = jnp.concatenate([tile, pad], axis=0).astype(jnp.bfloat16)

    for fetch in fetches:
        fetch.wait()
    for p in range(pairs):
        for h, (f, j) in enumerate(members(p)):
            at = (2 * j + 1) * HEAD_DIM
            vt[p, h * HEAD_DIM : (h + 1) * HEAD_DIM, :] = cbuf[f, :, at : at + HEAD_DIM].T

    lane = lax.broadcasted_iota(jnp.int32, (1, lanes), 1)
    lane_token = lax.rem(lane, tokens)
    first = lane < rows

    def by_lane(p, value):
        (f0, _), (f1, _) = members(p)
        return jnp.where(first, value(f0), value(f1))

    def attend(origin, p):
        tile = qbuf[origin, p]
        blank = jnp.zeros((rows, HEAD_DIM), jnp.bfloat16)
        spread = jnp.concatenate(
            [
                jnp.concatenate([tile[:rows], blank], axis=1),
                jnp.concatenate([blank, tile[rows:]], axis=1),
            ],
            axis=0,
        )
        keys = jnp.concatenate(
            [cbuf[f, :, 2 * j * HEAD_DIM : (2 * j + 1) * HEAD_DIM] for f, j in members(p)], axis=1
        )
        score = lax.dot_general(keys, spread, NT, preferred_element_type=jnp.float32) * factor
        score_new = lax.dot_general(kf[p], spread, NT, preferred_element_type=jnp.float32) * factor
        live = by_lane(p, lambda f: placed_ref[f, 0] * blocks_ref[f, 0] * BLOCK)
        slot = lax.broadcasted_iota(jnp.int32, (slots, lanes), 0)
        score = jnp.where(slot < live, score, HIDDEN)
        row = lax.broadcasted_iota(jnp.int32, (FRESH_ROWS, lanes), 0)
        counted = (row < tokens) & (me * tokens + row <= origin * tokens + lane_token)
        score_new = jnp.where(counted, score_new, HIDDEN)
        top = jnp.maximum(
            jnp.max(score, axis=0, keepdims=True), jnp.max(score_new, axis=0, keepdims=True)
        )
        top = jnp.maximum(top, FLOOR)
        weight = jnp.exp2(score - top)
        weight_new = jnp.exp2(score_new - top)
        total = jnp.sum(weight, axis=0, keepdims=True) + jnp.sum(weight_new, axis=0, keepdims=True)
        both = jnp.dot(vt[p], weight.astype(jnp.bfloat16), preferred_element_type=jnp.float32)
        both = both + lax.dot_general(
            vf[p], weight_new.astype(jnp.bfloat16), TN, preferred_element_type=jnp.float32
        )
        numer = jnp.where(first, both[:HEAD_DIM], both[HEAD_DIM:])
        pn[origin, p] = numer
        ps[origin, p, 0:1] = top
        ps[origin, p, 1:2] = total

    def kept(d, p):
        return pn[d, p], ps[d, p, 0:1], ps[d, p, 1:2]

    def arrived(slot, p):
        numer = ci[slot, p].astype(jnp.int32).astype(jnp.float32) * cis[slot, p, 2:3]
        return numer, cis[slot, p, 0:1], cis[slot, p, 1:2]

    def merge(one, two):
        top = jnp.maximum(one[1], two[1])
        a = jnp.exp2(one[1] - top)
        b = jnp.exp2(two[1] - top)
        return a * one[0] + b * two[0], top, a * one[2] + b * two[2]

    def pack(d, p, part):
        numer, top, total = part
        reach = jnp.maximum(jnp.max(jnp.abs(numer), axis=0, keepdims=True), 1e-30)
        co[d, p] = jnp.round(numer * (STEPS / reach)).astype(jnp.int32).astype(jnp.int16)
        row = lax.broadcasted_iota(jnp.int32, (8, lanes), 0)
        cos[d, p] = jnp.where(row == 0, top, jnp.where(row == 1, total, reach * (1.0 / STEPS)))

    def chain_copies(d, c, side):
        target = me + 1 if side == 0 else me - 1
        slot = d if side == 0 else jnp.where(d == target, n, d)
        part = pl.ds(c * per, per)
        where = dict(device_id={"inst": target}, device_id_type=MESH)
        return (
            pltpu.make_async_remote_copy(
                src_ref=co.at[d, part], dst_ref=ci.at[slot, part],
                send_sem=c_send.at[d, c], recv_sem=c_recv.at[slot, c], **where
            ),
            pltpu.make_async_remote_copy(
                src_ref=cos.at[d, part], dst_ref=cis.at[slot, part],
                send_sem=s_send.at[d, c], recv_sem=s_recv.at[slot, c], **where
            ),
        )

    def chain_arrival(slot, c):
        part = pl.ds(c * per, per)
        pltpu.make_async_copy(ci.at[slot, part], ci.at[slot, part], c_recv.at[slot, c]).wait()
        pltpu.make_async_copy(cis.at[slot, part], cis.at[slot, part], s_recv.at[slot, c]).wait()

    for p in range(pairs):
        attend(me, p)

    def advance(t, carry):
        for c in range(CHUNKS):
            for side in range(2):
                origin = me - t if side == 0 else me + t
                there = (t < n) & (origin >= 0 if side == 0 else origin < n)

                @pl.when(there)
                def _():
                    q_copy(origin, c, side).wait_recv()

                    @pl.when(me + 1 < n if side == 0 else me > 0)
                    def _():
                        q_copy(origin, c, side).start()

                    for p in range(c * per, (c + 1) * per):
                        attend(origin, p)

            for side in range(2):
                place = me if side == 0 else n - 1 - me
                far = t - place
                d = far if side == 0 else n - 1 - far

                @pl.when((far > place) & (far < n))
                def _():
                    @pl.when(place == 0)
                    def _():
                        for p in range(c * per, (c + 1) * per):
                            pack(d, p, kept(d, p))

                    @pl.when(place > 0)
                    def _():
                        chain_arrival(d, c)
                        for p in range(c * per, (c + 1) * per):
                            pack(d, p, merge(kept(d, p), arrived(d, p)))

                    for copy in chain_copies(d, c, side):
                        copy.start()
        return carry

    lax.fori_loop(1, 2 * n - 1, advance, 0)

    for k in range(1, n):
        source = lax.rem(me + n - k, n)
        pltpu.make_async_copy(pi.at[source], pi.at[source], o_recv.at[source]).wait()
    gathered = [pi[i].astype(jnp.float32) for i in range(n)]
    for a in range(width_kv // HEAD_DIM):
        column = jnp.concatenate([x[a * tokens : (a + 1) * tokens] for x in gathered], axis=0)
        owned_ref[0, 0, :, a * HEAD_DIM : (a + 1) * HEAD_DIM] = column.astype(jnp.bfloat16)

    for c in range(CHUNKS):
        for slot, there in ((me, me > 0), (n, me + 1 < n)):
            @pl.when(there)
            def _():
                chain_arrival(slot, c)
                for p in range(c * per, (c + 1) * per):
                    numer, top, total = merge(kept(me, p), arrived(slot, p))
                    pn[me, p] = numer
                    ps[me, p, 0:1] = top
                    ps[me, p, 1:2] = total

        for p in range(c * per, (c + 1) * per):
            numer, _, total = kept(me, p)
            span = by_lane(p, lambda f: span_ref[f])
            result = jnp.where(me * tokens + lane_token < span, numer / total, 0.0).T
            for h, (f, j) in enumerate(members(p)):
                for g in range(group):
                    at = (j * group + g) * HEAD_DIM
                    start = h * rows + g * tokens
                    att_ref[f, :, at : at + HEAD_DIM] = result[start : start + tokens].astype(
                        jnp.bfloat16
                    )

    for k in range(1, n):
        parcel(k).wait_send()
    for c in range(CHUNKS):
        for side in range(2):
            @pl.when(me + 1 < n if side == 0 else me > 0)
            def _():
                q_copy(me, c, side).wait_send()

    def drain(t, carry):
        for c in range(CHUNKS):
            for side in range(2):
                origin = me - t if side == 0 else me + t
                onward = me + 1 < n if side == 0 else me > 0

                @pl.when((origin >= 0 if side == 0 else origin < n) & onward)
                def _():
                    q_copy(origin, c, side).wait_send()

                d = me + t if side == 0 else me - t

                @pl.when(d < n if side == 0 else d >= 0)
                def _():
                    for copy in chain_copies(d, c, side):
                        copy.wait_send()
        return carry

    lax.fori_loop(1, n, drain, 0)


def body(queries, tool_key_value, cache, placed, blocks, span_len, owner):
    n = lax.axis_size("inst")
    forks, tokens, width = queries.shape
    width_kv = tool_key_value.shape[2]
    slots = cache.shape[1]
    kv_heads = width_kv // (2 * HEAD_DIM)
    group = width // (kv_heads * HEAD_DIM)
    pairs = forks * kv_heads // 2
    lanes = 2 * group * tokens
    parcel = (n, tokens * width_kv // HEAD_DIM, HEAD_DIM)
    bf16, f32, i16 = jnp.bfloat16, jnp.float32, jnp.int16
    vmem, smem = pltpu.VMEM, pltpu.SMEM
    dma = pltpu.SemaphoreType.DMA
    work = n * pairs * slots * lanes
    return pl.pallas_call(
        functools.partial(kernel, n),
        out_shape=(
            jax.ShapeDtypeStruct(queries.shape, bf16),
            jax.ShapeDtypeStruct((1, 1, n * tokens, width_kv), bf16),
        ),
        in_specs=[
            pl.BlockSpec(memory_space=vmem),
            pl.BlockSpec(memory_space=vmem),
            pl.BlockSpec(memory_space=pl.ANY),
        ]
        + [pl.BlockSpec(memory_space=smem)] * 4,
        out_specs=(pl.BlockSpec(memory_space=vmem), pl.BlockSpec(memory_space=vmem)),
        scratch_shapes=[
            vmem(cache.shape, bf16),
            vmem((pairs, 2 * HEAD_DIM, slots), bf16),
            vmem((pairs, FRESH_ROWS, 2 * HEAD_DIM), bf16),
            vmem((pairs, FRESH_ROWS, 2 * HEAD_DIM), bf16),
            vmem((n, pairs, lanes, HEAD_DIM), bf16),
            vmem((n, pairs, HEAD_DIM, lanes), f32),
            vmem((n, pairs, 8, lanes), f32),
            vmem((n + 1, pairs, HEAD_DIM, lanes), i16),
            vmem((n + 1, pairs, 8, lanes), f32),
            vmem((n, pairs, HEAD_DIM, lanes), i16),
            vmem((n, pairs, 8, lanes), f32),
            vmem(parcel, bf16),
            vmem(parcel, bf16),
            dma((forks,)),
            dma((2, n, CHUNKS)),
            dma((n, CHUNKS)),
            dma((n, CHUNKS)),
            dma((n, CHUNKS)),
            dma((n + 1, CHUNKS)),
            dma((n + 1, CHUNKS)),
            dma((n,)),
            dma((n,)),
        ],
        compiler_params=pltpu.CompilerParams(
            collective_id=0, has_side_effects=True, vmem_limit_bytes=48 * 1024 * 1024
        ),
        cost_estimate=pl.CostEstimate(
            flops=work * 8 * HEAD_DIM, bytes_accessed=2 * cache.size, transcendentals=work
        ),
    )(queries, tool_key_value, cache, placed, blocks, span_len, owner)


def solution(mesh):
    return jax.shard_map(
        body,
        mesh=mesh,
        in_specs=(
            P(("groups", "rep"), "inst", "tp"),
            P(("groups", "rep"), "inst", "tp"),
            P(("groups", "rep"), "inst", "tp"),
            P(("groups", "rep"), "inst"),
            P(("groups", "rep"), "inst"),
            P(("groups", "rep")),
            P(("groups", "rep")),
        ),
        out_specs=(P(("groups", "rep"), "inst", "tp"), P(("groups", "inst"), "rep", None, "tp")),
        check_vma=False,
    )
```

time: 79.7 us -> 40.4 us (0.51)
  Pallas kernels: 0 us -> 31.9 us
  starting transfers between devices: 23.2 us -> 0 us
  waiting for transfers between devices: 14.7 us -> 0 us
  matrix products: 12.8 us -> 0 us
  other arithmetic: 12.6 us -> 0 us
  local copies, waits for them, and re-layouts: 14.8 us -> 7.63 us
    pallas_call x0 -> x1, Pallas kernels: none -> 31.9 us  [body(): pl.pallas_call(functools.partial(kernel, n), out_shape=(jax.ShapeDtypeStr...]
    ppermute x14 -> x0, starting transfers between devices: 18.2 us -> none  [passed_along(): lax.ppermute(shard, axis, [(i, (i + by) % size) for i in range(size)])]
    dot_general x17 -> x0, matrix products: 12.8 us -> none  [the longest x4 5.18 us: block_partial(): jnp.einsum('fcjgp,fpjd->fcjgd', weight_old.astype(jnp.bfloat16), value_ca...]
    ppermute x14 -> x0, waiting for transfers between devices: 10.9 us -> none  [passed_along(): lax.ppermute(shard, axis, [(i, (i + by) % size) for i in range(size)])]
    all_to_all x1 -> x0, starting transfers between devices: 5.09 us -> none  [body(): lax.all_to_all(parcels, 'inst', split_axis=0, concat_axis=0, tiled=True)]
    add x11 -> x0, other arithmetic: 4.84 us -> none  [the longest x3 4.21 us: merge_parts(): scale_one * sum_one + scale_two * sum_two]
    all_to_all x1 -> x0, waiting for transfers between devices: 3.72 us -> none  [body(): lax.all_to_all(parcels, 'inst', split_axis=0, concat_axis=0, tiled=True)]
    lt x6 -> x0, other arithmetic: 3.52 us -> none  [the longest x5 2.78 us: block_partial(): mask_old = (slots[None, :] < live_len[:, None])[:, None, None, None, :]]
  transfers between devices with their start and end apart: 15 -> 0, of which waited for: 7 -> 0; matrix products, arithmetic and copies ran while one was open for 23% -> 0% of each run, Pallas kernels for 0% -> 0%
where the time goes in v1:
time: 40.4 us; the launch traced here: 40.1 us
  Pallas kernels  31.9 us (79%)
  local copies, waits for them, and re-layouts  7.63 us (19%)
  between operations  0.64 us (2%)
    pallas_call x1, Pallas kernels, body(): pl.pallas_call(functools.partial(kernel, n), out_shape=(jax.ShapeDtypeStr...  31.9 us
    unnamed x14, local copies, waits for them, and re-layouts  7.63 us

profile of v1, /device:TPU:0, one launch (start us, length us, event | category | flops | bytes accessed | tf_op | source)
XLA Modules:
  0.0 40.1 jit_solution(1668014417904651403)
XLA Ops:
  0.6 0.7 %copy.9.placed_ref = s32[2,1]{1,0:T(2,128)S(1)} copy(s32[2,1]{0,1:T(1,128)} %param.10) | data formatting | bytes 16 | tf_op args[3]
  1.4 0.7 %copy.10.blocks_ref = s32[2,1]{1,0:T(2,128)S(1)} copy(s32[2,1]{0,1:T(1,128)} %param.11) | data formatting | bytes 16 | tf_op args[4]
  2.1 0.0 copy-start
  2.1 1.9 %copy-done = bf16[2,768,1024]{2,1,0:T(8,128)(2,1)S(1)} copy-done((bf16[2,768,1024]{2,1,0:T(8,128)(2,1)S(1)}, bf16[2,768,1024]{2,1,0:T(8,128)(2,1)}, u32[]{:S(2)}) %copy-start) | copy-done | bytes 3145752
  4.0 0.0 copy-start.1
  4.0 0.9 %copy-done.1 = bf16[2,8,4096]{2,1,0:T(8,128)(2,1)S(1)} copy-done((bf16[2,8,4096]{2,1,0:T(8,128)(2,1)S(1)}, bf16[2,8,4096]{2,1,0:T(8,128)(2,1)}, u32[]{:S(2)}) %copy-start.1) | copy-done | bytes 131096
  4.9 0.0 copy-start.2
  4.9 0.8 %copy-done.2 = bf16[2,8,1024]{2,1,0:T(8,128)(2,1)S(1)} copy-done((bf16[2,8,1024]{2,1,0:T(8,128)(2,1)S(1)}, bf16[2,8,1024]{2,1,0:T(8,128)(2,1)}, u32[]{:S(2)}) %copy-start.2) | copy-done | bytes 32792
  5.7 0.0 copy-start.3
  5.7 0.7 %copy-done.3 = s32[2]{0:T(128)S(1)} copy-done((s32[2]{0:T(128)S(1)}, s32[2]{0:T(128)}, u32[]{:S(2)}) %copy-start.3) | copy-done | bytes 32
  6.3 0.0 copy-start.4
  6.3 0.7 %copy-done.4 = s32[2]{0:T(128)S(1)} copy-done((s32[2]{0:T(128)S(1)}, s32[2]{0:T(128)}, u32[]{:S(2)}) %copy-start.4) | copy-done | bytes 32
  7.0 31.9 %shard_map.86 = (bf16[2,8,4096]{2,1,0:T(8,128)(2,1)S(1)}, bf16[1,1,32,1024]{3,2,1,0:T(8,128)(2,1)S(1)}) custom-call(bf16[2,8,4096]{2,1,0:T(8,128)(2,1)S(1)} %copy-done.1, bf16[2,8,1024]{2,1,0:T(8,128)(2,1)S(1)} %copy-done.2, bf16[2,768,1024]{2,1,0:T(8,128)(2,1)S(1)} %copy-done, s32[2,1]{1,0:T(2,128)S(1)} %copy.9.placed_ref, s32[2,1]{1,0:T(2,128)S(1)} %copy.10.blocks_ref, ...), custom_call_target="tpu_custom_call" | custom-call | flops 1610612736 | bytes 3145728 | tf_op jit(solution)/shard_map/pallas_call | solution.py:327
  38.9 0.7 %copy.13 = bf16[2,8,4096]{2,1,0:T(8,128)(2,1)} copy(bf16[2,8,4096]{2,1,0:T(8,128)(2,1)S(1)} %get-tuple-element.4) | data formatting | bytes 262144
  39.5 0.6 %copy.14 = bf16[1,1,32,1024]{3,2,1,0:T(8,128)(2,1)} copy(bf16[1,1,32,1024]{3,2,1,0:T(8,128)(2,1)S(1)} %get-tuple-element.5) | data formatting | bytes 131072
Async XLA Ops:
  2.1 1.9 %copy-start = (bf16[2,768,1024]{2,1,0:T(8,128)(2,1)S(1)}, bf16[2,768,1024]{2,1,0:T(8,128)(2,1)}, u32[]{:S(2)}) copy-start(bf16[2,768,1024]{2,1,0:T(8,128)(2,1)} %cache_ref.1) | copy-start | bytes 9437188
  4.0 0.9 %copy-start.1 = (bf16[2,8,4096]{2,1,0:T(8,128)(2,1)S(1)}, bf16[2,8,4096]{2,1,0:T(8,128)(2,1)}, u32[]{:S(2)}) copy-start(bf16[2,8,4096]{2,1,0:T(8,128)(2,1)} %q_ref.1) | copy-start | bytes 393220
  4.9 0.8 %copy-start.2 = (bf16[2,8,1024]{2,1,0:T(8,128)(2,1)S(1)}, bf16[2,8,1024]{2,1,0:T(8,128)(2,1)}, u32[]{:S(2)}) copy-start(bf16[2,8,1024]{2,1,0:T(8,128)(2,1)} %kv_ref.1) | copy-start | bytes 98308
  5.7 0.7 %copy-start.3 = (s32[2]{0:T(128)S(1)}, s32[2]{0:T(128)}, u32[]{:S(2)}) copy-start(s32[2]{0:T(128)} %span_ref.1) | copy-start | bytes 28
  6.3 0.7 %copy-start.4 = (s32[2]{0:T(128)S(1)}, s32[2]{0:T(128)}, u32[]{:S(2)}) copy-start(s32[2]{0:T(128)} %owner_ref.1) | copy-start | bytes 28

commit v2 on v1

--- a/solution.py
+++ b/solution.py
@@ -22,8 +22,10 @@
 
 
 def kernel(
-    n, q_ref, kv_ref, cache_ref, placed_ref, blocks_ref, span_ref, owner_ref,
-    att_ref, owned_ref,
+    n, q_hbm, kv_hbm, cache_ref, placed_hbm, blocks_hbm, span_hbm, owner_hbm,
+    att_hbm, owned_hbm,
+    att_ref, owned_ref, output_sem,
+    q_ref, kv_ref, placed_ref, blocks_ref, span_ref, owner_ref, input_sem,
     cbuf, vt, kf, vf, qbuf, pn, ps, ci, cis, co, cos, po, pi,
     cache_sem, q_send, q_recv, c_send, s_send, c_recv, s_recv, o_send, o_recv,
 ):
@@ -39,6 +41,17 @@
     factor = LOG2E / math.sqrt(HEAD_DIM)
     me = lax.axis_index("inst")
 
+    inputs = [
+        pltpu.make_async_copy(source, target, input_sem.at[k])
+        for k, (source, target) in enumerate(
+            (
+                (q_hbm, q_ref), (kv_hbm, kv_ref), (placed_hbm, placed_ref),
+                (blocks_hbm, blocks_ref), (span_hbm, span_ref), (owner_hbm, owner_ref),
+            )
+        )
+    ]
+    for fetch in inputs:
+        fetch.start()
     fetches = [
         pltpu.make_async_copy(cache_ref.at[f], cbuf.at[f], cache_sem.at[f])
         for f in range(forks)
@@ -55,6 +68,7 @@
     def members(p):
         return [(u // kv_heads, u % kv_heads) for u in (2 * p, 2 * p + 1)]
 
+    inputs[0].wait()
     for p in range(pairs):
         parts = []
         for f, j in members(p):
@@ -79,6 +93,8 @@
             def _():
                 q_copy(me, c, side).start()
 
+    for fetch in inputs[1:]:
+        fetch.wait()
     for i in range(n):
         chosen = None
         for f in range(forks):
@@ -100,9 +116,6 @@
             device_id={"inst": target}, device_id_type=MESH,
         )
 
-    for k in range(1, n):
-        parcel(k).start()
-
     for p in range(pairs):
         for ref, shift in ((kf, 0), (vf, HEAD_DIM)):
             both = [
@@ -128,42 +141,82 @@
         (f0, _), (f1, _) = members(p)
         return jnp.where(first, value(f0), value(f1))
 
-    def attend(origin, p):
+    def spread(origin, p):
         tile = qbuf[origin, p]
         blank = jnp.zeros((rows, HEAD_DIM), jnp.bfloat16)
-        spread = jnp.concatenate(
+        return jnp.concatenate(
             [
                 jnp.concatenate([tile[:rows], blank], axis=1),
                 jnp.concatenate([blank, tile[rows:]], axis=1),
             ],
             axis=0,
         )
+
+    def scores(origins, p):
+        against = jnp.concatenate([spread(origin, p) for origin in origins], axis=0)
         keys = jnp.concatenate(
             [cbuf[f, :, 2 * j * HEAD_DIM : (2 * j + 1) * HEAD_DIM] for f, j in members(p)], axis=1
         )
-        score = lax.dot_general(keys, spread, NT, preferred_element_type=jnp.float32) * factor
-        score_new = lax.dot_general(kf[p], spread, NT, preferred_element_type=jnp.float32) * factor
-        live = by_lane(p, lambda f: placed_ref[f, 0] * blocks_ref[f, 0] * BLOCK)
-        slot = lax.broadcasted_iota(jnp.int32, (slots, lanes), 0)
-        score = jnp.where(slot < live, score, HIDDEN)
+        score = lax.dot_general(keys, against, NT, preferred_element_type=jnp.float32)
+        score_new = lax.dot_general(kf[p], against, NT, preferred_element_type=jnp.float32)
+        return score, score_new
+
+    def weigh(origin, p, score, score_new):
+        live = by_lane(p, lambda f: placed_ref[f] * blocks_ref[f])
+        tiles = [score[a : a + BLOCK].reshape(-1, 8, lanes) for a in range(0, slots, BLOCK)]
         row = lax.broadcasted_iota(jnp.int32, (FRESH_ROWS, lanes), 0)
         counted = (row < tokens) & (me * tokens + row <= origin * tokens + lane_token)
-        score_new = jnp.where(counted, score_new, HIDDEN)
-        top = jnp.maximum(
-            jnp.max(score, axis=0, keepdims=True), jnp.max(score_new, axis=0, keepdims=True)
-        )
-        top = jnp.maximum(top, FLOOR)
-        weight = jnp.exp2(score - top)
+        score_new = jnp.where(counted, score_new * factor, HIDDEN)
+        top = jnp.max(score_new.reshape(-1, 8, lanes), axis=0)
+        for b, tile in enumerate(tiles):
+            top = jnp.maximum(top, jnp.where(b < live, jnp.max(tile, axis=0) * factor, HIDDEN))
+        top = jnp.maximum(jnp.max(top, axis=0, keepdims=True), FLOOR)
         weight_new = jnp.exp2(score_new - top)
-        total = jnp.sum(weight, axis=0, keepdims=True) + jnp.sum(weight_new, axis=0, keepdims=True)
-        both = jnp.dot(vt[p], weight.astype(jnp.bfloat16), preferred_element_type=jnp.float32)
-        both = both + lax.dot_general(
-            vf[p], weight_new.astype(jnp.bfloat16), TN, preferred_element_type=jnp.float32
-        )
-        numer = jnp.where(first, both[:HEAD_DIM], both[HEAD_DIM:])
-        pn[origin, p] = numer
-        ps[origin, p, 0:1] = top
-        ps[origin, p, 1:2] = total
+        total = jnp.sum(weight_new.reshape(-1, 8, lanes), axis=0)
+        weights = []
+        for b, tile in enumerate(tiles):
+            shift = jnp.where(b < live, top, -HIDDEN)
+            weight = jnp.exp2(tile * factor - shift[None])
+            total = total + jnp.sum(weight, axis=0)
+            weights.append(weight.reshape(BLOCK, lanes).astype(jnp.bfloat16))
+        total = jnp.sum(total, axis=0, keepdims=True)
+        return jnp.concatenate(weights, axis=0), weight_new.astype(jnp.bfloat16), top, total
+
+    def partials(origins, p, score, score_new):
+        parts = [
+            weigh(
+                origin, p, score[:, k * lanes : (k + 1) * lanes],
+                score_new[:, k * lanes : (k + 1) * lanes],
+            )
+            for k, origin in enumerate(origins)
+        ]
+        weight = jnp.concatenate([part[0] for part in parts], axis=1)
+        weight_new = jnp.concatenate([part[1] for part in parts], axis=1)
+        both = jnp.dot(vt[p], weight, preferred_element_type=jnp.float32)
+        both = both + lax.dot_general(vf[p], weight_new, TN, preferred_element_type=jnp.float32)
+        return [
+            (
+                jnp.where(
+                    first,
+                    both[:HEAD_DIM, k * lanes : (k + 1) * lanes],
+                    both[HEAD_DIM:, k * lanes : (k + 1) * lanes],
+                ),
+                part[2],
+                part[3],
+            )
+            for k, part in enumerate(parts)
+        ]
+
+    def attend(origins, after=None):
+        ahead = scores(origins, 0)
+        for p in range(pairs):
+            now = ahead
+            if p + 1 < pairs:
+                ahead = scores(origins, p + 1)
+            for origin, part in zip(origins, partials(origins, p, *now)):
+                pn[origin, p], ps[origin, p, 0:1], ps[origin, p, 1:2] = part
+            if after is not None:
+                after(p)
 
     def kept(d, p):
         return pn[d, p], ps[d, p, 0:1], ps[d, p, 1:2]
@@ -186,8 +239,8 @@
         cos[d, p] = jnp.where(row == 0, top, jnp.where(row == 1, total, reach * (1.0 / STEPS)))
 
     def chain_copies(d, c, side):
-        target = me + 1 if side == 0 else me - 1
-        slot = d if side == 0 else jnp.where(d == target, n, d)
+        target = me + 1 - 2 * side
+        slot = jnp.where((d == target) & (side == 1), n, d)
         part = pl.ds(c * per, per)
         where = dict(device_id={"inst": target}, device_id_type=MESH)
         return (
@@ -206,25 +259,58 @@
         pltpu.make_async_copy(ci.at[slot, part], ci.at[slot, part], c_recv.at[slot, c]).wait()
         pltpu.make_async_copy(cis.at[slot, part], cis.at[slot, part], s_recv.at[slot, c]).wait()
 
-    for p in range(pairs):
-        attend(me, p)
+    at_end = (me == 0) | (me == n - 1)
+    end_side = jnp.where(me == 0, 0, 1)
+
+    def relay(t, chunks):
+        for side in range(2):
+            origin = me - t if side == 0 else me + t
+            there = origin >= 0 if side == 0 else origin < n
+            onward = me + 1 < n if side == 0 else me > 0
+
+            @pl.when(there & onward)
+            def _():
+                for c in chunks:
+                    q_copy(origin, c, side).wait_recv()
+                    q_copy(origin, c, side).start()
+
+    def relay_part(t, parts):
+        size = -(-CHUNKS // parts)
+        return lambda p: relay(t, range(min(p * size, CHUNKS), min((p + 1) * size, CHUNKS)))
+
+    attend([me], relay_part(1, pairs))
 
     def advance(t, carry):
-        for c in range(CHUNKS):
-            for side in range(2):
-                origin = me - t if side == 0 else me + t
-                there = (t < n) & (origin >= 0 if side == 0 else origin < n)
-
-                @pl.when(there)
+        @pl.when(t == n - 1)
+        def _():
+            for k in range(1, n):
+                parcel(k).start()
+
+        @pl.when(at_end & (t < n))
+        def _():
+            origin = me + t * (1 - 2 * end_side)
+            for c in range(CHUNKS):
+                q_copy(origin, c, 0).wait_recv()
+                for p in range(c * per, (c + 1) * per):
+                    pack(origin, p, partials([origin], p, *scores([origin], p))[0])
+                for copy in chain_copies(origin, c, end_side):
+                    copy.start()
+
+        @pl.when(jnp.logical_not(at_end))
+        def _():
+            before, beyond = me - t >= 0, me + t < n
+
+            @pl.when(before & beyond)
+            def _():
+                attend([me - t, me + t], relay_part(t + 1, pairs // 2))
+
+            @pl.when(jnp.logical_not(before & beyond))
+            def _():
+                @pl.when(before | beyond)
                 def _():
-                    q_copy(origin, c, side).wait_recv()
-
-                    @pl.when(me + 1 < n if side == 0 else me > 0)
-                    def _():
-                        q_copy(origin, c, side).start()
-
-                    for p in range(c * per, (c + 1) * per):
-                        attend(origin, p)
+                    attend([jnp.where(before, me - t, me + t)])
+
+                relay(t + 1, range(CHUNKS))
 
             for side in range(2):
                 place = me if side == 0 else n - 1 - me
@@ -233,19 +319,13 @@
 
                 @pl.when((far > place) & (far < n))
                 def _():
-                    @pl.when(place == 0)
-                    def _():
-                        for p in range(c * per, (c + 1) * per):
-                            pack(d, p, kept(d, p))
-
-                    @pl.when(place > 0)
-                    def _():
+                    for c in range(CHUNKS):
                         chain_arrival(d, c)
                         for p in range(c * per, (c + 1) * per):
                             pack(d, p, merge(kept(d, p), arrived(d, p)))
-
-                    for copy in chain_copies(d, c, side):
-                        copy.start()
+                        for copy in chain_copies(d, c, side):
+                            copy.start()
+
         return carry
 
     lax.fori_loop(1, 2 * n - 1, advance, 0)
@@ -257,6 +337,8 @@
     for a in range(width_kv // HEAD_DIM):
         column = jnp.concatenate([x[a * tokens : (a + 1) * tokens] for x in gathered], axis=0)
         owned_ref[0, 0, :, a * HEAD_DIM : (a + 1) * HEAD_DIM] = column.astype(jnp.bfloat16)
+    results = [pltpu.make_async_copy(owned_ref, owned_hbm, output_sem.at[2 * pairs])]
+    results[0].start()
 
     for c in range(CHUNKS):
         for slot, there in ((me, me > 0), (n, me + 1 < n)):
@@ -280,7 +362,15 @@
                     att_ref[f, :, at : at + HEAD_DIM] = result[start : start + tokens].astype(
                         jnp.bfloat16
                     )
-
+                span = pl.ds(j * group * HEAD_DIM, group * HEAD_DIM)
+                result_copy = pltpu.make_async_copy(
+                    att_ref.at[f, :, span], att_hbm.at[f, :, span], output_sem.at[2 * p + h]
+                )
+                result_copy.start()
+                results.append(result_copy)
+
+    for result_copy in results:
+        result_copy.wait()
     for k in range(1, n):
         parcel(k).wait_send()
     for c in range(CHUNKS):
@@ -308,6 +398,17 @@
         return carry
 
     lax.fori_loop(1, n, drain, 0)
+
+
+def hand_over(attended, owned, attended_out, owned_out, sem):
+    copies = [
+        pltpu.make_async_copy(attended, attended_out, sem.at[0]),
+        pltpu.make_async_copy(owned, owned_out, sem.at[1]),
+    ]
+    for copy in copies:
+        copy.start()
+    for copy in copies:
+        copy.wait()
 
 
 def body(queries, tool_key_value, cache, placed, blocks, span_len, owner):
@@ -324,20 +425,28 @@
     vmem, smem = pltpu.VMEM, pltpu.SMEM
     dma = pltpu.SemaphoreType.DMA
     work = n * pairs * slots * lanes
-    return pl.pallas_call(
+    attended, owned = pl.pallas_call(
         functools.partial(kernel, n),
         out_shape=(
             jax.ShapeDtypeStruct(queries.shape, bf16),
             jax.ShapeDtypeStruct((1, 1, n * tokens, width_kv), bf16),
         ),
         in_specs=[
-            pl.BlockSpec(memory_space=vmem),
-            pl.BlockSpec(memory_space=vmem),
-            pl.BlockSpec(memory_space=pl.ANY),
+            pl.BlockSpec(memory_space=pltpu.HBM)
         ]
-        + [pl.BlockSpec(memory_space=smem)] * 4,
-        out_specs=(pl.BlockSpec(memory_space=vmem), pl.BlockSpec(memory_space=vmem)),
+        * 7,
+        out_specs=(pl.BlockSpec(memory_space=pltpu.HBM),) * 2,
         scratch_shapes=[
+            vmem(queries.shape, bf16),
+            vmem((1, 1, n * tokens, width_kv), bf16),
+            dma((2 * pairs + 1,)),
+            vmem(queries.shape, bf16),
+            vmem(tool_key_value.shape, bf16),
+            smem((forks,), jnp.int32),
+            smem((forks,), jnp.int32),
+            smem((forks,), jnp.int32),
+            smem((forks,), jnp.int32),
+            dma((6,)),
             vmem(cache.shape, bf16),
             vmem((pairs, 2 * HEAD_DIM, slots), bf16),
             vmem((pairs, FRESH_ROWS, 2 * HEAD_DIM), bf16),
@@ -362,12 +471,23 @@
             dma((n,)),
         ],
         compiler_params=pltpu.CompilerParams(
-            collective_id=0, has_side_effects=True, vmem_limit_bytes=48 * 1024 * 1024
+            collective_id=0, has_side_effects=True, vmem_limit_bytes=63 * 1024 * 1024
         ),
         cost_estimate=pl.CostEstimate(
             flops=work * 8 * HEAD_DIM, bytes_accessed=2 * cache.size, transcendentals=work
         ),
-    )(queries, tool_key_value, cache, placed, blocks, span_len, owner)
+    )(queries, tool_key_value, cache, placed.reshape(-1), blocks.reshape(-1), span_len, owner)
+    return pl.pallas_call(
+        hand_over,
+        out_shape=(
+            jax.ShapeDtypeStruct(attended.shape, bf16),
+            jax.ShapeDtypeStruct(owned.shape, bf16),
+        ),
+        in_specs=[pl.BlockSpec(memory_space=pltpu.HBM)] * 2,
+        out_specs=(pl.BlockSpec(memory_space=pltpu.HBM),) * 2,
+        scratch_shapes=[dma((2,))],
+        compiler_params=pltpu.CompilerParams(vmem_limit_bytes=63 * 1024 * 1024),
+    )(attended, owned)
 
 
 def solution(mesh):

time: 40.4 us -> 36.6 us (0.906)
  local copies, waits for them, and re-layouts: 7.63 us -> 0 us
  Pallas kernels: 31.9 us -> 35.8 us
    unnamed x14 -> x0, local copies, waits for them, and re-layouts: 7.63 us -> none
    pallas_call x0 -> x1, Pallas kernels: none -> 7.08 us  [body(): pl.pallas_call(hand_over, out_shape=(jax.ShapeDtypeStruct(attended.shape,...]
    pallas_call x1, Pallas kernels: 31.9 us -> 28.7 us  [body(): pl.pallas_call(functools.partial(kernel, n), out_shape=(jax.ShapeDtypeStr...]
where the time goes in v2:
time: 36.6 us; the launch traced here: 36.4 us
  Pallas kernels  35.8 us (98%)
  between operations  0.64 us (2%)
    pallas_call x1, Pallas kernels, body(): pl.pallas_call(functools.partial(kernel, n), out_shape=(jax.ShapeDtypeStr...  28.7 us
    pallas_call x1, Pallas kernels, body(): pl.pallas_call(hand_over, out_shape=(jax.ShapeDtypeStruct(attended.shape,...  7.08 us

profile of v2, /device:TPU:0, one launch (start us, length us, event | category | flops | bytes accessed | tf_op | source)
XLA Modules:
  0.0 36.4 jit_solution(3115934962894301520)
XLA Ops:
  0.6 28.7 %shard_map.86 = (bf16[2,8,4096]{2,1,0:T(8,128)(2,1)}, bf16[1,1,32,1024]{3,2,1,0:T(8,128)(2,1)}) custom-call(bf16[2,8,4096]{2,1,0:T(8,128)(2,1)} %q_hbm.1, bf16[2,8,1024]{2,1,0:T(8,128)(2,1)} %kv_hbm.1, bf16[2,768,1024]{2,1,0:T(8,128)(2,1)} %cache_ref.1, s32[2]{0:T(128)} %bitcast.2, s32[2]{0:T(128)} %bitcast.3, s32[2]{0:T(128)} %span_hbm.1, s32[2]{0:T(128)} %owner_hbm.1), custom_call_target="tpu_custom_call" | custom-call | flops 1610612736 | bytes 3145728 | tf_op jit(solution)/shard_map/pallas_call | solution.py:428
  29.3 7.1 %shard_map.87 = (bf16[2,8,4096]{2,1,0:T(8,128)(2,1)}, bf16[1,1,32,1024]{3,2,1,0:T(8,128)(2,1)}) custom-call(bf16[2,8,4096]{2,1,0:T(8,128)(2,1)} %get-tuple-element.4.attended, bf16[1,1,32,1024]{3,2,1,0:T(8,128)(2,1)} %get-tuple-element.5.owned), custom_call_target="tpu_custom_call" | custom-call | tf_op jit(solution)/shard_map/pallas_call | solution.py:480

commit v3 on v2

--- a/solution.py
+++ b/solution.py
@@ -23,8 +23,7 @@
 
 def kernel(
     n, q_hbm, kv_hbm, cache_ref, placed_hbm, blocks_hbm, span_hbm, owner_hbm,
-    att_hbm, owned_hbm,
-    att_ref, owned_ref, output_sem,
+    att_ref, owned_ref,
     q_ref, kv_ref, placed_ref, blocks_ref, span_ref, owner_ref, input_sem,
     cbuf, vt, kf, vf, qbuf, pn, ps, ci, cis, co, cos, po, pi,
     cache_sem, q_send, q_recv, c_send, s_send, c_recv, s_recv, o_send, o_recv,
@@ -289,10 +288,18 @@
         @pl.when(at_end & (t < n))
         def _():
             origin = me + t * (1 - 2 * end_side)
+
+            def arrive(c):
+                q_copy(origin, c, 0).wait_recv()
+                return [(p, scores([origin], p)) for p in range(c * per, (c + 1) * per)]
+
+            ahead = arrive(0)
             for c in range(CHUNKS):
-                q_copy(origin, c, 0).wait_recv()
-                for p in range(c * per, (c + 1) * per):
-                    pack(origin, p, partials([origin], p, *scores([origin], p))[0])
+                now = ahead
+                if c + 1 < CHUNKS:
+                    ahead = arrive(c + 1)
+                for p, score in now:
+                    pack(origin, p, partials([origin], p, *score)[0])
                 for copy in chain_copies(origin, c, end_side):
                     copy.start()
 
@@ -337,8 +344,6 @@
     for a in range(width_kv // HEAD_DIM):
         column = jnp.concatenate([x[a * tokens : (a + 1) * tokens] for x in gathered], axis=0)
         owned_ref[0, 0, :, a * HEAD_DIM : (a + 1) * HEAD_DIM] = column.astype(jnp.bfloat16)
-    results = [pltpu.make_async_copy(owned_ref, owned_hbm, output_sem.at[2 * pairs])]
-    results[0].start()
 
     for c in range(CHUNKS):
         for slot, there in ((me, me > 0), (n, me + 1 < n)):
@@ -362,15 +367,7 @@
                     att_ref[f, :, at : at + HEAD_DIM] = result[start : start + tokens].astype(
                         jnp.bfloat16
                     )
-                span = pl.ds(j * group * HEAD_DIM, group * HEAD_DIM)
-                result_copy = pltpu.make_async_copy(
-                    att_ref.at[f, :, span], att_hbm.at[f, :, span], output_sem.at[2 * p + h]
-                )
-                result_copy.start()
-                results.append(result_copy)
-
-    for result_copy in results:
-        result_copy.wait()
+
     for k in range(1, n):
         parcel(k).wait_send()
     for c in range(CHUNKS):
@@ -400,15 +397,9 @@
     lax.fori_loop(1, n, drain, 0)
 
 
-def hand_over(attended, owned, attended_out, owned_out, sem):
-    copies = [
-        pltpu.make_async_copy(attended, attended_out, sem.at[0]),
-        pltpu.make_async_copy(owned, owned_out, sem.at[1]),
-    ]
-    for copy in copies:
-        copy.start()
-    for copy in copies:
-        copy.wait()
+def hand_over(attended, owned, attended_out, owned_out):
+    attended_out[...] = attended[...]
+    owned_out[...] = owned[...]
 
 
 def body(queries, tool_key_value, cache, placed, blocks, span_len, owner):
@@ -435,11 +426,8 @@
             pl.BlockSpec(memory_space=pltpu.HBM)
         ]
         * 7,
-        out_specs=(pl.BlockSpec(memory_space=pltpu.HBM),) * 2,
+        out_specs=(pl.BlockSpec(memory_space=vmem), pl.BlockSpec(memory_space=vmem)),
         scratch_shapes=[
-            vmem(queries.shape, bf16),
-            vmem((1, 1, n * tokens, width_kv), bf16),
-            dma((2 * pairs + 1,)),
             vmem(queries.shape, bf16),
             vmem(tool_key_value.shape, bf16),
             smem((forks,), jnp.int32),
@@ -483,9 +471,8 @@
             jax.ShapeDtypeStruct(attended.shape, bf16),
             jax.ShapeDtypeStruct(owned.shape, bf16),
         ),
-        in_specs=[pl.BlockSpec(memory_space=pltpu.HBM)] * 2,
-        out_specs=(pl.BlockSpec(memory_space=pltpu.HBM),) * 2,
-        scratch_shapes=[dma((2,))],
+        in_specs=[pl.BlockSpec(memory_space=vmem)] * 2,
+        out_specs=(pl.BlockSpec(memory_space=vmem),) * 2,
         compiler_params=pltpu.CompilerParams(vmem_limit_bytes=63 * 1024 * 1024),
     )(attended, owned)
 

time: 36.6 us -> 31 us (0.85)
  Pallas kernels: 35.8 us -> 30.2 us
    pallas_call x1, Pallas kernels: 7.08 us -> 1.59 us  [body(): pl.pallas_call(hand_over, out_shape=(jax.ShapeDtypeStruct(attended.shape,...]
where the time goes in v3:
time: 31 us; the launch traced here: 30.8 us
  Pallas kernels  30.2 us (97%)
  between operations  0.64 us (2%)
    pallas_call x1, Pallas kernels, body(): pl.pallas_call(functools.partial(kernel, n), out_shape=(jax.ShapeDtypeStr...  28.6 us
    pallas_call x1, Pallas kernels, body(): pl.pallas_call(hand_over, out_shape=(jax.ShapeDtypeStruct(attended.shape,...  1.59 us

profile of v3, /device:TPU:0, one launch (start us, length us, event | category | flops | bytes accessed | tf_op | source)
XLA Modules:
  0.0 30.8 jit_solution(5444331820618159910)
XLA Ops:
  0.6 28.6 %shard_map.86 = (bf16[2,8,4096]{2,1,0:T(8,128)(2,1)}, bf16[1,1,32,1024]{3,2,1,0:T(8,128)(2,1)}) custom-call(bf16[2,8,4096]{2,1,0:T(8,128)(2,1)} %q_hbm.1, bf16[2,8,1024]{2,1,0:T(8,128)(2,1)} %kv_hbm.1, bf16[2,768,1024]{2,1,0:T(8,128)(2,1)} %cache_ref.1, s32[2]{0:T(128)} %bitcast.2, s32[2]{0:T(128)} %bitcast.3, s32[2]{0:T(128)} %span_hbm.1, s32[2]{0:T(128)} %owner_hbm.1), custom_call_target="tpu_custom_call" | custom-call | flops 1610612736 | bytes 3145728 | tf_op jit(solution)/shard_map/pallas_call | solution.py:419
  29.2 1.6 %shard_map.87 = (bf16[2,8,4096]{2,1,0:T(8,128)(2,1)}, bf16[1,1,32,1024]{3,2,1,0:T(8,128)(2,1)}) custom-call(bf16[2,8,4096]{2,1,0:T(8,128)(2,1)} %get-tuple-element.4.attended, bf16[1,1,32,1024]{3,2,1,0:T(8,128)(2,1)} %get-tuple-element.5.owned), custom_call_target="tpu_custom_call" | custom-call | tf_op jit(solution)/shard_map/pallas_call | solution.py:468

commit v4 on v3

--- a/solution.py
+++ b/solution.py
@@ -275,8 +275,18 @@
 
     def relay_part(t, parts):
         size = -(-CHUNKS // parts)
-        return lambda p: relay(t, range(min(p * size, CHUNKS), min((p + 1) * size, CHUNKS)))
-
+        return lambda p: relay(
+            t, range(min(1 + p * size, CHUNKS), min(1 + (p + 1) * size, CHUNKS))
+        )
+
+    def chain_step(d, c, side):
+        chain_arrival(d, c)
+        for p in range(c * per, (c + 1) * per):
+            pack(d, p, merge(kept(d, p), arrived(d, p)))
+        for copy in chain_copies(d, c, side):
+            copy.start()
+
+    relay(1, range(1))
     attend([me], relay_part(1, pairs))
 
     def advance(t, carry):
@@ -309,13 +319,24 @@
 
             @pl.when(before & beyond)
             def _():
+                relay(t + 1, range(1))
                 attend([me - t, me + t], relay_part(t + 1, pairs // 2))
 
             @pl.when(jnp.logical_not(before & beyond))
             def _():
                 @pl.when(before | beyond)
                 def _():
-                    attend([jnp.where(before, me - t, me + t)])
+                    origin = jnp.where(before, me - t, me + t)
+                    side = jnp.where(before, 1, 0)
+                    prompt = jnp.where(before, me == n - 2, me == 1)
+
+                    def after(p):
+                        if (p + 1) % per == 0:
+                            @pl.when(prompt)
+                            def _():
+                                chain_step(origin, p // per, side)
+
+                    attend([origin], after)
 
                 relay(t + 1, range(CHUNKS))
 
@@ -324,14 +345,12 @@
                 far = t - place
                 d = far if side == 0 else n - 1 - far
 
-                @pl.when((far > place) & (far < n))
+                done = (place == 1) & (far > place + 1)
+
+                @pl.when((far > place) & (far < n) & jnp.logical_not(done))
                 def _():
                     for c in range(CHUNKS):
-                        chain_arrival(d, c)
-                        for p in range(c * per, (c + 1) * per):
-                            pack(d, p, merge(kept(d, p), arrived(d, p)))
-                        for copy in chain_copies(d, c, side):
-                            copy.start()
+                        chain_step(d, c, side)
 
         return carry
 

time: 31 us -> 32.9 us (1.061)
  Pallas kernels: 30.2 us -> 32.1 us
    pallas_call x1, Pallas kernels: 28.6 us -> 30.5 us  [body(): pl.pallas_call(functools.partial(kernel, n), out_shape=(jax.ShapeDtypeStr...]
where the time goes in v4:
time: 32.9 us; the launch traced here: 32.7 us
  Pallas kernels  32.1 us (98%)
  between operations  0.64 us (2%)
    pallas_call x1, Pallas kernels, body(): pl.pallas_call(functools.partial(kernel, n), out_shape=(jax.ShapeDtypeStr...  30.5 us
    pallas_call x1, Pallas kernels, body(): pl.pallas_call(hand_over, out_shape=(jax.ShapeDtypeStruct(attended.shape,...  1.59 us

profile of v4, /device:TPU:0, one launch (start us, length us, event | category | flops | bytes accessed | tf_op | source)
XLA Modules:
  0.0 32.7 jit_solution(2181196436954447572)
XLA Ops:
  0.6 30.5 %shard_map.86 = (bf16[2,8,4096]{2,1,0:T(8,128)(2,1)}, bf16[1,1,32,1024]{3,2,1,0:T(8,128)(2,1)}) custom-call(bf16[2,8,4096]{2,1,0:T(8,128)(2,1)} %q_hbm.1, bf16[2,8,1024]{2,1,0:T(8,128)(2,1)} %kv_hbm.1, bf16[2,768,1024]{2,1,0:T(8,128)(2,1)} %cache_ref.1, s32[2]{0:T(128)} %bitcast.2, s32[2]{0:T(128)} %bitcast.3, s32[2]{0:T(128)} %span_hbm.1, s32[2]{0:T(128)} %owner_hbm.1), custom_call_target="tpu_custom_call" | custom-call | flops 1610612736 | bytes 3145728 | tf_op jit(solution)/shard_map/pallas_call | solution.py:438
  31.1 1.6 %shard_map.87 = (bf16[2,8,4096]{2,1,0:T(8,128)(2,1)}, bf16[1,1,32,1024]{3,2,1,0:T(8,128)(2,1)}) custom-call(bf16[2,8,4096]{2,1,0:T(8,128)(2,1)} %get-tuple-element.4.attended, bf16[1,1,32,1024]{3,2,1,0:T(8,128)(2,1)} %get-tuple-element.5.owned), custom_call_target="tpu_custom_call" | custom-call | tf_op jit(solution)/shard_map/pallas_call | solution.py:487

commit v5 on v4

--- a/solution.py
+++ b/solution.py
@@ -290,7 +290,7 @@
     attend([me], relay_part(1, pairs))
 
     def advance(t, carry):
-        @pl.when(t == n - 1)
+        @pl.when(t == n // 2)
         def _():
             for k in range(1, n):
                 parcel(k).start()
@@ -326,17 +326,7 @@
             def _():
                 @pl.when(before | beyond)
                 def _():
-                    origin = jnp.where(before, me - t, me + t)
-                    side = jnp.where(before, 1, 0)
-                    prompt = jnp.where(before, me == n - 2, me == 1)
-
-                    def after(p):
-                        if (p + 1) % per == 0:
-                            @pl.when(prompt)
-                            def _():
-                                chain_step(origin, p // per, side)
-
-                    attend([origin], after)
+                    attend([jnp.where(before, me - t, me + t)])
 
                 relay(t + 1, range(CHUNKS))
 
@@ -345,9 +335,8 @@
                 far = t - place
                 d = far if side == 0 else n - 1 - far
 
-                done = (place == 1) & (far > place + 1)
-
-                @pl.when((far > place) & (far < n) & jnp.logical_not(done))
+
+                @pl.when((far > place) & (far < n))
                 def _():
                     for c in range(CHUNKS):
                         chain_step(d, c, side)

time: 32.9 us -> 31.4 us (0.954)
  Pallas kernels: 32.1 us -> 30.6 us
    pallas_call x1, Pallas kernels: 30.5 us -> 29 us  [body(): pl.pallas_call(functools.partial(kernel, n), out_shape=(jax.ShapeDtypeStr...]
where the time goes in v5:
time: 31.4 us; the launch traced here: 31.2 us
  Pallas kernels  30.6 us (97%)
  between operations  0.64 us (2%)
    pallas_call x1, Pallas kernels, body(): pl.pallas_call(functools.partial(kernel, n), out_shape=(jax.ShapeDtypeStr...  29 us
    pallas_call x1, Pallas kernels, body(): pl.pallas_call(hand_over, out_shape=(jax.ShapeDtypeStruct(attended.shape,...  1.59 us

profile of v5, /device:TPU:0, one launch (start us, length us, event | category | flops | bytes accessed | tf_op | source)
XLA Modules:
  0.0 31.2 jit_solution(806326955022538431)
XLA Ops:
  0.6 29.0 %shard_map.86 = (bf16[2,8,4096]{2,1,0:T(8,128)(2,1)}, bf16[1,1,32,1024]{3,2,1,0:T(8,128)(2,1)}) custom-call(bf16[2,8,4096]{2,1,0:T(8,128)(2,1)} %q_hbm.1, bf16[2,8,1024]{2,1,0:T(8,128)(2,1)} %kv_hbm.1, bf16[2,768,1024]{2,1,0:T(8,128)(2,1)} %cache_ref.1, s32[2]{0:T(128)} %bitcast.2, s32[2]{0:T(128)} %bitcast.3, s32[2]{0:T(128)} %span_hbm.1, s32[2]{0:T(128)} %owner_hbm.1), custom_call_target="tpu_custom_call" | custom-call | flops 1610612736 | bytes 3145728 | tf_op jit(solution)/shard_map/pallas_call | solution.py:427
  29.6 1.6 %shard_map.87 = (bf16[2,8,4096]{2,1,0:T(8,128)(2,1)}, bf16[1,1,32,1024]{3,2,1,0:T(8,128)(2,1)}) custom-call(bf16[2,8,4096]{2,1,0:T(8,128)(2,1)} %get-tuple-element.4.attended, bf16[1,1,32,1024]{3,2,1,0:T(8,128)(2,1)} %get-tuple-element.5.owned), custom_call_target="tpu_custom_call" | custom-call | tf_op jit(solution)/shard_map/pallas_call | solution.py:476
